TPU v7x, 512 devices: a whole 4x8x8 slice. The times are simulated.
512 devices in a mesh: section: 16 (over y_lo, z), tensor: 32 (over x, y_hi, core).
Axes of the slice: x: 4, y: 8 (y_hi: 4, y_lo: 2; y = y_hi * 2 + y_lo), z: 8, core: 2. Of those that a mesh axis runs over, the one named last changes fastest.
Arguments:
- x_down: bfloat16 [2, 16, 128, 4096], P(None, 'section', 'tensor'), may hold values from -6 to 6
- x_up: bfloat16 [2, 16, 128, 4096], P(None, 'section', 'tensor'), may hold values from -6 to 6
- g_down: bfloat16 [16, 128, 4096], P('section', 'tensor'), may hold values from -6 to 6
- g_up: bfloat16 [16, 128, 4096], P('section', 'tensor'), may hold values from -6 to 6
- loss_grad: bfloat16 [2, 128, 4096], P(None, 'tensor'), may hold values from -6 to 6
- w_in: bfloat16 [16, 4096, 4096], P('section', None, 'tensor'), may hold values from -1 to 1
- w_out: bfloat16 [16, 4096, 4096], P('section', 'tensor'), may hold values from -0.09375 to 0.09375
- gain: bfloat16 [16, 4096], P('section'), may hold values from 0.5 to 1.5
- retention: bfloat16 [16, 4096], P('section', 'tensor'), may hold values from 0.8984375 to 0.9921875
- layer_kind: int32 [16], replicated, may hold values from 0 to 1, as said below
Outputs:
- gx_down: bfloat16 [16, 128, 4096], P('section', 'tensor')
- gx_up: bfloat16 [16, 128, 4096], P('section', 'tensor')
- grad_in: bfloat16 [16, 4096, 4096], P('section', None, 'tensor')
- grad_out: bfloat16 [16, 4096, 4096], P('section', 'tensor')
Inputs may be any that keep to these rules, and one draw needn't show every extreme that they name: `layer_kind`: each aligned group of 8 layers holds at least one attention layer and at least one recurrent layer.
All inputs are finite; a program needn't handle non-finite values.
Results may differ from a plain program's by a relative error of at most 0.039.
Values may be sent and summed in bfloat16 or wider, within the bound.
A program may use at most 128 MiB of HBM per device.

v0:
```python
import jax
import jax.numpy as jnp
from jax import lax
from jax.sharding import PartitionSpec as P

EPSILON = 1e-05


def for_sending(value):
    return jax.tree.map(lambda a: a.astype(jnp.bfloat16) if a.dtype == jnp.float32 else a, value)


def from_behind(value, axis, steps):
    count = lax.axis_size(axis)
    first, last = (max(0, -steps), min(count, count - steps))
    return lax.ppermute(value, axis, [(source, source + steps) for source in range(first, last)])


def combine_steps(earlier, following):
    first_decay, first_state = earlier
    next_decay, next_state = following
    return (first_decay * next_decay, next_decay * first_state + next_state)


def mix_head(projected, rates, kind):

    def recurrent(values_in):
        decay = jnp.broadcast_to(rates, values_in.shape)
        states = lax.associative_scan(combine_steps, (decay, (1.0 - rates) * values_in), axis=0)[1]
        return states * jax.nn.silu(values_in)

    def attend(values_in):
        half_width = values_in.shape[-1] // 2
        queries = values_in[:, :half_width]
        key_part = values_in[:, half_width:]
        scores = lax.dot_general(
            queries, key_part, (((1,), (1,)), ((), ())), precision=lax.Precision.HIGHEST
        ) * half_width ** (-0.5)
        length_now = values_in.shape[0]
        causal = jnp.arange(length_now)[:, None] >= jnp.arange(length_now)[None, :]
        scores = jnp.where(causal, scores, -1e30)
        row_max = jnp.max(scores, axis=-1, keepdims=True)
        weights = jnp.exp(scores - row_max)
        weights = weights / jnp.sum(weights, axis=-1, keepdims=True)
        return jnp.dot(weights, values_in, precision=lax.Precision.HIGHEST)

    return lax.cond(kind == 1, attend, recurrent, projected)


def contract_last(left, right):
    return lax.dot_general(
        left, right, (((1,), (1,)), ((), ())), preferred_element_type=jnp.float32
    )


def contract_pair(first_left, second_left, first_right, second_right):
    left = jnp.stack([first_left, second_left])
    right = jnp.stack([first_right, second_right])
    return lax.dot_general(
        left, right, (((0, 1), (0, 1)), ((), ())), preferred_element_type=jnp.float32
    )


def layer_backward(x_rows, grad_rows, params, kind):
    w_in_l, w_out_l, gain_l, rate_l = params
    row_count = x_rows.shape[0]
    x_float = x_rows.astype(jnp.float32)
    recip = lax.rsqrt(jnp.mean(x_float * x_float, axis=-1, keepdims=True) + EPSILON)
    gain_f = gain_l.astype(jnp.float32)
    normed_rows = (x_float * recip * gain_f).astype(jnp.bfloat16)
    normed, grad_y = (
        lax.all_gather(normed_rows, "tensor", axis=0, tiled=True),
        lax.all_gather(grad_rows, "tensor", axis=0, tiled=True),
    )
    projected = jnp.dot(normed, w_in_l, preferred_element_type=jnp.float32)
    width = projected.shape[1]
    rates = rate_l.astype(jnp.float32).reshape(1, width)
    mixed, mix_pull = jax.vjp(lambda values_in: mix_head(values_in, rates, kind), projected)
    mixed_b = mixed.astype(jnp.bfloat16)
    grad_mixed = contract_last(grad_y, w_out_l)
    grad_proj = mix_pull(grad_mixed)[0].astype(jnp.bfloat16)
    summed = lax.psum(contract_last(grad_proj, w_in_l).astype(jnp.bfloat16), "tensor").astype(
        jnp.float32
    )
    row_start = lax.axis_index("tensor") * row_count
    grad_normed = lax.dynamic_slice_in_dim(summed, row_start, row_count, 0)
    scaled = grad_normed * gain_f
    grad_x = recip * scaled - x_float * recip**3 * jnp.mean(
        scaled * x_float, axis=-1, keepdims=True
    )
    result = (grad_rows.astype(jnp.float32) + grad_x).astype(jnp.bfloat16)
    return (result, (normed, grad_proj, mixed_b, grad_y))


def weight_sums(first_saved, second_saved):
    grad_w_in = contract_pair(first_saved[0], second_saved[0], first_saved[1], second_saved[1])
    grad_w_out = contract_pair(first_saved[2], second_saved[2], first_saved[3], second_saved[3])
    return (grad_w_in.astype(jnp.bfloat16), grad_w_out.astype(jnp.bfloat16))


def flatten_parts(parts, sections):
    return tuple((piece.reshape(sections, -1) for piece in parts))


def restore_parts(flat, parts):
    return tuple((piece.reshape(model.shape) for piece, model in zip(flat, parts)))


def fetch_mirror(parts, sections):
    spread = lax.all_to_all(
        for_sending(flatten_parts(parts, sections)),
        "section",
        split_axis=0,
        concat_axis=0,
        tiled=True,
    )
    flipped = tuple((jnp.flip(piece, 0) for piece in spread))
    collected = jax.tree.map(
        lambda part, own: part.astype(own.dtype),
        lax.all_to_all(for_sending(flipped), "section", split_axis=0, concat_axis=0, tiled=True),
        flipped,
    )
    return restore_parts(collected, parts)


def return_mirror(parts, sections):
    spread = lax.all_to_all(
        for_sending(flatten_parts(parts, sections)),
        "section",
        split_axis=0,
        concat_axis=0,
        tiled=True,
    )
    flipped = tuple((jnp.flip(piece, 0) for piece in spread))
    collected = jax.tree.map(
        lambda part, own: part.astype(own.dtype),
        lax.all_to_all(for_sending(flipped), "section", split_axis=0, concat_axis=0, tiled=True),
        flipped,
    )
    return restore_parts(collected, parts)


def body(x_down, x_up, g_down, g_up, loss_grad, w_in, w_out, gain, retention, layer_kind):
    sections = lax.axis_size("section")
    position = lax.axis_index("section")
    final_section = sections - 1
    own_params = (w_in[0], w_out[0], gain[0], retention[0])
    own_kind = lax.dynamic_index_in_dim(layer_kind, position, 0, keepdims=False)
    mirror_kind = lax.dynamic_index_in_dim(layer_kind, final_section - position, 0, keepdims=False)
    mirror_params = fetch_mirror(own_params, sections)
    down_first, down_saved_one = layer_backward(x_down[0, 0], g_down[0], own_params, own_kind)
    up_first, up_saved_one = layer_backward(x_up[0, 0], g_up[0], mirror_params, mirror_kind)
    from_above = from_behind(down_first, "section", -1)
    from_below = from_behind(up_first, "section", 1)
    down_next = jnp.where(position == final_section, loss_grad[0], from_above)
    up_next = jnp.where(position == 0, loss_grad[1], from_below)
    down_final, down_saved_two = layer_backward(x_down[1, 0], down_next, own_params, own_kind)
    up_final, up_saved_two = layer_backward(x_up[1, 0], up_next, mirror_params, mirror_kind)
    partner_in, partner_out = return_mirror(weight_sums(up_saved_one, up_saved_two), sections)
    own_in, own_out = weight_sums(down_saved_one, down_saved_two)
    grad_in = (own_in.astype(jnp.float32) + partner_in.astype(jnp.float32)).astype(jnp.bfloat16)
    grad_out = (own_out.astype(jnp.float32) + partner_out.astype(jnp.float32)).astype(jnp.bfloat16)
    return (down_final[None], up_final[None], grad_in[None], grad_out[None])


def solution(mesh):
    return jax.shard_map(
        body,
        mesh=mesh,
        in_specs=(
            P(None, "section", "tensor", None),
            P(None, "section", "tensor", None),
            P("section", "tensor", None),
            P("section", "tensor", None),
            P(None, "tensor", None),
            P("section", None, "tensor"),
            P("section", "tensor", None),
            P("section", None),
            P("section", "tensor"),
            P(),
        ),
        out_specs=(
            P("section", "tensor", None),
            P("section", "tensor", None),
            P("section", None, "tensor"),
            P("section", "tensor", None),
        ),
        check_vma=False,
    )
```

profile of v0, /device:TPU:1, one launch (start us, length us, event | category | flops | bytes accessed | tf_op | source)
XLA Modules:
  0.0 1512.9 jit_solution(6567628706065679449)
XLA Ops:
  13.6 12.0 all-to-all-start
  37.1 6.3 all-to-all-done.2
  62.4 7.0 reduce.17
  71.0 7.6 all-to-all-start.6
  80.1 8.0 reduce.15
  90.7 12.4 all-to-all-done.6
  103.1 7.8 all-to-all-start.4
  118.1 89.7 %rev.24 = bf16[16,32768]{1,0:T(8,128)(2,1)S(1)} reverse(bf16[16,32768]{1,0:T(8,128)(2,1)} %bitcast.291), dimensions={0} | reverse | bytes 2097152 | tf_op jit(solution)/shard_map/jit(_flip)/rev | solution.py:117
  210.8 7.5 all-to-all-start.7
  226.8 89.7 %rev.23 = bf16[16,32768]{1,0:T(8,128)(2,1)S(1)} reverse(bf16[16,32768]{1,0:T(8,128)(2,1)} %bitcast.292), dimensions={0} | reverse | bytes 2097152 | tf_op jit(solution)/shard_map/jit(_flip)/rev | solution.py:117
  319.5 7.5 all-to-all-start.5
  331.0 14.4 conditional.8
  349.2 30.2 %conditional.9 = (bf16[128,128]{1,0:T(8,128)(2,1)S(1)}) conditional(s32[]{:T(128)} %bitcast.35, (f32[128,128]{1,0:T(8,128)S(1)}, f32[128,128]{1,0:T(8,128)S(1)}, f32[128,128]{1,0:T(8,128)S(1)}, f32[128,128]{1,0:T(8,128)S(1)}, f32[128,128]{1,0:T(8,128)}, /*index=5*/f32[1,128]{1,0:T(1,128)}, f32[128,128]{1,0:T(8,128)}, f32[63,128]{1,0:T(8,128)}, ...), branch_computations={%region_6.7_spmd, %region_7.10_spmd} | conditional | flops 75792512 | bytes 3054698 | solution.py:47
  392.5 7.7 reduce.3
  407.6 8.7 reduce.2
  420.4 22.7 %conditional.12 = (f32[1,128]{1,0:T(1,128)}, f32[64,128]{1,0:T(8,128)}, f32[32,128]{1,0:T(8,128)}, f32[16,128]{1,0:T(8,128)}, f32[8,128]{1,0:T(8,128)}, /*index=...) conditional(s32[]{:T(128)} %bitcast.49, ...), branch_computations={%region_25.26_spmd, %region_26.30_spmd} | conditional | flops 37945216 | bytes 2524605 | solution.py:47
  443.1 34.2 %conditional.13 = (bf16[128,128]{1,0:T(8,128)(2,1)S(1)}) conditional(s32[]{:T(128)} %bitcast.49, (f32[128,128]{1,0:T(8,128)}, f32[128,128]{1,0:T(8,128)S(1)}, f32[128,128]{1,0:T(8,128)S(1)}, f32[128,128]{1,0:T(8,128)S(1)}, f32[128,128]{1,0:T(8,128)S(1)}, /*index=5*/f32[1,128]{1,0:T(1,128)}, f32[128,128]{1,0:T(8,128)}, f32[63,128]{1,0:T(8,128)}, ...), branch_computations={%region_30.31_spmd, %region_31.34_spmd} | conditional | flops 75792512 | bytes 3316870 | solution.py:47
  479.0 298.0 %all-reduce.199.cloned.1.call-done = (bf16[128,4096]{1,0:T(8,128)(2,1)}, bf16[128,4096]{1,0:T(8,128)(2,1)}) async-done(((bf16[128,4096]{1,0:T(8,128)(2,1)}, bf16[128,4096]{1,0:T(8,128)(2,1)}), (bf16[128,4096]{1,0:T(8,128)(2,1)}, bf16[128,4096]{1,0:T(8,128)(2,1)})) %all-reduce.199.cloned.1.call-update) | async-done | bytes 2097168 | tf_op jit(solution)/shard_map/psum | solution.py:82
  796.9 42.1 %all-gather.29.cloned.1.call-done = bf16[32,4,4096]{2,1,0:T(4,128)(2,1)} async-done(((bf16[1,4,4096]{2,1,0:T(4,128)(2,1)}), bf16[32,4,4096]{2,1,0:T(4,128)(2,1)}) %all-gather.29.cloned.1.call-update) | async-done | bytes 1048592 | tf_op jit(solution)/shard_map/all_gather | solution.py:72
  847.2 22.9 %conditional.14 = (f32[1,128]{1,0:T(1,128)}, f32[64,128]{1,0:T(8,128)}, f32[32,128]{1,0:T(8,128)}, f32[16,128]{1,0:T(8,128)}, f32[8,128]{1,0:T(8,128)}, /*index=...) conditional(s32[]{:T(128)} %bitcast.49, ...), branch_computations={%region_37.38_spmd, %region_38.42_spmd} | conditional | flops 37945216 | bytes 2526681 | solution.py:47
  870.1 27.7 %all-gather.31.cloned.1.call-done = bf16[32,4,4096]{2,1,0:T(4,128)(2,1)} async-done(((bf16[1,4,4096]{2,1,0:T(4,128)(2,1)}), bf16[32,4,4096]{2,1,0:T(4,128)(2,1)}) %all-gather.31.cloned.1.call-update) | async-done | bytes 1048592 | tf_op jit(solution)/shard_map/all_gather | solution.py:73
  901.9 81.3 %conditional.15 = (bf16[128,128]{1,0:T(8,128)(2,1)}) conditional(s32[]{:T(128)} %bitcast.49, (f32[128,128]{1,0:T(8,128)S(1)}, f32[128,128]{1,0:T(8,128)S(1)}, f32[128,128]{1,0:T(8,128)S(1)}, f32[128,128]{1,0:T(8,128)S(1)}, f32[128,128]{1,0:T(8,128)}, /*index=5*/f32[1,128]{1,0:T(1,128)}, f32[128,128]{1,0:T(8,128)}, f32[63,128]{1,0:T(8,128)}, ...), branch_computations={%region_42.43_spmd, %region_43.46_spmd} | conditional | flops 75792512 | bytes 2923598 | solution.py:47
  992.0 9.3 reduce.19
  1004.0 7.4 all-to-all-start.8
  1023.4 9.3 reduce.21
  1037.0 7.0 all-to-all-start.10
  1047.8 23.4 %conditional.10 = (f32[1,128]{1,0:T(1,128)}, f32[64,128]{1,0:T(8,128)}, f32[32,128]{1,0:T(8,128)}, f32[16,128]{1,0:T(8,128)}, f32[8,128]{1,0:T(8,128)}, /*index=...) conditional(s32[]{:T(128)} %bitcast.35, ...), branch_computations={%region_13.14_spmd, %region_14.18_spmd} | conditional | flops 37945216 | bytes 2526681 | solution.py:47
  1084.2 77.0 %rev.25 = bf16[16,32768]{1,0:T(8,128)(2,1)} reverse(bf16[16,32768]{1,0:T(8,128)(2,1)S(1)} %bitcast.293), dimensions={0} | reverse | bytes 2097152 | tf_op jit(solution)/shard_map/jit(_flip)/rev | solution.py:134
  1165.6 7.7 all-to-all-start.9
  1198.4 7.5 all-to-all-start.11
  1213.9 264.2 %all-reduce.197.cloned.1.call-done = (bf16[128,4096]{1,0:T(8,128)(2,1)}, bf16[128,4096]{1,0:T(8,128)(2,1)}) async-done(((bf16[128,4096]{1,0:T(8,128)(2,1)}, bf16[128,4096]{1,0:T(8,128)(2,1)}), (bf16[128,4096]{1,0:T(8,128)(2,1)}, bf16[128,4096]{1,0:T(8,128)(2,1)})) %all-reduce.197.cloned.1.call-update) | async-done | bytes 2097168 | tf_op jit(solution)/shard_map/psum | solution.py:82
  1490.0 7.3 convert_reduce_fusion
  (910 shorter events, 459.8 us)
Async XLA Ops:
  7.2 322.0 %all-gather.21.cloned.1.call-start = ((), (), s32[]{:S(2)}) async-start(), calls=%async_computation.14 | async-start | bytes 1081344 | tf_op jit(solution)/shard_map/all_gather | solution.py:72
  12.8 318.1 %copy-start.46 = (f32[1,128]{1,0:T(1,128)}, f32[1,128]{1,0:T(1,128)S(1)}, u32[]{:S(2)}) copy-start(f32[1,128]{1,0:T(1,128)S(1)} %get-tuple-element.1761) | copy-start | bytes 1540
  13.6 19.2 %all-to-all-start = ((bf16[16,1,8]{2,1,0:T(2,128)(2,1)}), bf16[16,1,8]{2,1,0:T(2,128)(2,1)S(1)}, u32[]{:S(2)}, u32[]{:S(2)}) async-start(bf16[16,1,8]{2,1,0:T(2,128)(2,1)} %all_to_all.114), calls=%async_computation | async-start | bytes 16384 | tf_op jit(solution)/shard_map/all_to_all | solution.py:110
  32.8 10.7 all-to-all-start.2
  43.4 10.7 all-to-all-start.1
  54.1 16.9 %all-to-all-start.3 = ((bf16[16,2,128]{2,1,0:T(2,128)(2,1)}), bf16[16,2,128]{2,1,0:T(2,128)(2,1)S(1)}, u32[]{:S(2)}, u32[]{:S(2)}) async-start(bf16[16,2,128]{2,1,0:T(2,128)(2,1)} %reshape.341), calls=%async_computation.3 | async-start | bytes 16384 | tf_op jit(solution)/shard_map/all_to_all | solution.py:120
  71.0 32.0 %all-to-all-start.6 = ((bf16[16,2,16384]{2,1,0:T(2,128)(2,1)}), bf16[16,2,16384]{2,1,0:T(2,128)(2,1)}, u32[]{:S(2)}, u32[]{:S(2)}) async-start(bf16[16,2,16384]{2,1,0:T(2,128)(2,1)} %reshape.347), calls=%async_computation.6 | async-start | bytes 2097152 | tf_op jit(solution)/shard_map/all_to_all | solution.py:110
  78.6 266.8 %all-gather.17.cloned.1.call-start = ((), (), s32[]{:S(2)}) async-start(), calls=%async_computation.12 | async-start | bytes 2162688 | tf_op jit(solution)/shard_map/all_gather | solution.py:73
  103.1 107.8 %all-to-all-start.4 = ((bf16[16,2,16384]{2,1,0:T(2,128)(2,1)}), bf16[16,2,16384]{2,1,0:T(2,128)(2,1)}, u32[]{:S(2)}, u32[]{:S(2)}) async-start(bf16[16,2,16384]{2,1,0:T(2,128)(2,1)} %reshape.343), calls=%async_computation.4 | async-start | bytes 2097152 | tf_op jit(solution)/shard_map/all_to_all | solution.py:110
  110.9 268.5 %all-gather.19.cloned.1.call-start = ((), (), s32[]{:S(2)}) async-start(), calls=%async_computation.13 | async-start | bytes 2162688 | tf_op jit(solution)/shard_map/all_gather | solution.py:73
  210.8 108.7 %all-to-all-start.7 = ((bf16[16,2,16384]{2,1,0:T(2,128)(2,1)}), bf16[16,2,16384]{2,1,0:T(2,128)(2,1)}, u32[]{:S(2)}, u32[]{:S(2)}) async-start(bf16[16,2,16384]{2,1,0:T(2,128)(2,1)} %reshape.349), calls=%async_computation.7 | async-start | bytes 2097152 | tf_op jit(solution)/shard_map/all_to_all | solution.py:120
  218.4 166.2 %all-gather.27.cloned.1.call-start = ((), (), s32[]{:S(2)}) async-start(), calls=%async_computation.17 | async-start | bytes 1081344 | tf_op jit(solution)/shard_map/all_gather | solution.py:72
  219.6 560.5 %copy-start.13 = (f32[16,1,256]{2,1,0:T(1,128)}, f32[16,1,256]{2,1,0:T(1,128)S(1)}, u32[]{:S(2)}) copy-start(f32[16,1,256]{2,1,0:T(1,128)S(1)} %convert_element_type.294) | copy-start | bytes 49156
  319.5 82.1 %all-to-all-start.5 = ((bf16[16,2,16384]{2,1,0:T(2,128)(2,1)}), bf16[16,2,16384]{2,1,0:T(2,128)(2,1)}, u32[]{:S(2)}, u32[]{:S(2)}) async-start(bf16[16,2,16384]{2,1,0:T(2,128)(2,1)} %reshape.345), calls=%async_computation.5 | async-start | bytes 2097152 | tf_op jit(solution)/shard_map/all_to_all | solution.py:120
  327.1 449.9 %all-reduce.199.cloned.1.call-start = ((), (), s32[]{:S(2)}) async-start(), calls=%async_computation.21 | async-start | bytes 4194304 | tf_op jit(solution)/shard_map/psum | solution.py:82
  477.4 302.7 %copy-start.31 = (bf16[1,4,4096]{2,1,0:T(4,128)(2,1)S(1)}, bf16[1,4,4096]{2,1,0:T(4,128)(2,1)}, u32[]{:S(2)}) copy-start(bf16[1,4,4096]{2,1,0:T(4,128)(2,1)} %param.29) | copy-start | bytes 98308
  477.4 302.7 %copy-start.85 = (f32[4]{0:T(128)S(1)}, f32[4]{0:T(128)}, u32[]{:S(2)}) copy-start(f32[4]{0:T(128)} %copy-done.84) | copy-start | bytes 52
  477.4 308.0 %copy-start.33 = (bf16[1,4,4096]{2,1,0:T(4,128)(2,1)S(1)}, bf16[1,4,4096]{2,1,0:T(4,128)(2,1)}, u32[]{:S(2)}) copy-start(bf16[1,4,4096]{2,1,0:T(4,128)(2,1)} %param.28) | copy-start | bytes 98308
  477.4 308.0 %copy-start.79 = (f32[4]{0:T(128)S(1)}, f32[4]{0:T(128)}, u32[]{:S(2)}) copy-start(f32[4]{0:T(128)} %copy-done.78) | copy-start | bytes 52
  477.4 308.0 %copy-start.92 = (f32[4]{0:T(128)S(1)}, f32[4]{0:T(128)}, u32[]{:S(2)}) copy-start(f32[4]{0:T(128)} %get-tuple-element.1758) | copy-start | bytes 52
  477.5 314.3 %copy-start.26 = (bf16[2,4,4096]{2,1,0:T(4,128)(2,1)S(1)}, bf16[2,4,4096]{2,1,0:T(4,128)(2,1)}, u32[]{:S(2)}) copy-start(bf16[2,4,4096]{2,1,0:T(4,128)(2,1)} %param.30) | copy-start | bytes 196612
  478.9 360.1 %all-gather.29.cloned.1.call-start = ((), (), s32[]{:S(2)}) async-start(), calls=%async_computation.18 | async-start | bytes 1081344 | tf_op jit(solution)/shard_map/all_gather | solution.py:72
  781.7 116.1 %all-gather.31.cloned.1.call-start = ((), (), s32[]{:S(2)}) async-start(), calls=%async_computation.19 | async-start | bytes 1081344 | tf_op jit(solution)/shard_map/all_gather | solution.py:73
  781.7 6.6 collective-permute-start.1
  787.1 4.6 collective-permute-start
  792.4 251.6 %all-gather.23.cloned.1.call-start = ((), (), s32[]{:S(2)}) async-start(), calls=%async_computation.15 | async-start | bytes 1081344 | tf_op jit(solution)/shard_map/all_gather | solution.py:72
  1004.0 33.0 %all-to-all-start.8 = ((bf16[16,2,16384]{2,1,0:T(2,128)(2,1)}), bf16[16,2,16384]{2,1,0:T(2,128)(2,1)}, u32[]{:S(2)}, u32[]{:S(2)}) async-start(bf16[16,2,16384]{2,1,0:T(2,128)(2,1)} %reshape.351), calls=%async_computation.8 | async-start | bytes 2097152 | tf_op jit(solution)/shard_map/all_to_all | solution.py:127
  1011.3 60.0 %all-gather.25.cloned.1.call-start = ((), (), s32[]{:S(2)}) async-start(), calls=%async_computation.16 | async-start | bytes 1081344 | tf_op jit(solution)/shard_map/all_gather | solution.py:73
  1037.0 128.6 %all-to-all-start.10 = ((bf16[16,2,16384]{2,1,0:T(2,128)(2,1)}), bf16[16,2,16384]{2,1,0:T(2,128)(2,1)}, u32[]{:S(2)}, u32[]{:S(2)}) async-start(bf16[16,2,16384]{2,1,0:T(2,128)(2,1)} %reshape.355), calls=%async_computation.10 | async-start | bytes 2097152 | tf_op jit(solution)/shard_map/all_to_all | solution.py:127
  1165.6 32.7 %all-to-all-start.9 = ((bf16[16,2,16384]{2,1,0:T(2,128)(2,1)}), bf16[16,2,16384]{2,1,0:T(2,128)(2,1)}, u32[]{:S(2)}, u32[]{:S(2)}) async-start(bf16[16,2,16384]{2,1,0:T(2,128)(2,1)} %reshape.353), calls=%async_computation.9 | async-start | bytes 2097152 | tf_op jit(solution)/shard_map/all_to_all | solution.py:137
  1173.4 304.8 %all-reduce.197.cloned.1.call-start = ((), (), s32[]{:S(2)}) async-start(), calls=%async_computation.20 | async-start | bytes 4194304 | tf_op jit(solution)/shard_map/psum | solution.py:82
  1198.4 290.5 %all-to-all-start.11 = ((bf16[16,2,16384]{2,1,0:T(2,128)(2,1)}), bf16[16,2,16384]{2,1,0:T(2,128)(2,1)S(1)}, u32[]{:S(2)}, u32[]{:S(2)}) async-start(bf16[16,2,16384]{2,1,0:T(2,128)(2,1)} %reshape.357), calls=%async_computation.11 | async-start | bytes 2097152 | tf_op jit(solution)/shard_map/all_to_all | solution.py:137
  (83 other events, 3393.3 us)
Sparse Core Ops, SparseCore 0:
  11.7 63.1 all-gather.20
  82.6 64.9 all-gather.16
  150.8 57.0 all-gather.18
  222.0 59.8 all-gather.26
  479.0 297.8 all-reduce.198
  781.8 57.1 all-gather.28
  842.6 55.1 all-gather.30
  902.0 55.1 all-gather.22
  1015.8 55.2 all-gather.24
  1179.0 299.1 all-reduce.196
where the time goes:
time: 1540 us; the launch traced here: 1510 us
  waiting for transfers between devices  673 us (44%)
  local copies, waits for them, and re-layouts  536 us (35%)
  other arithmetic  169 us (11%)
  starting transfers between devices  88.5 us (6%)
  matrix products  27.5 us (2%)
  between operations  17.1 us (1%)
    psum x2, waiting for transfers between devices, layer_backward(): lax.psum(contract_last(grad_proj, w_in_l).astype(jnp.bfloat16), 'tensor')  562 us
    rev x4, local copies, waits for them, and re-layouts, fetch_mirror(): flipped = tuple((jnp.flip(piece, 0) for piece in spread))  180 us
    unnamed x172, local copies, waits for them, and re-layouts  83.2 us
    rev x2, local copies, waits for them, and re-layouts, return_mirror(): flipped = tuple((jnp.flip(piece, 0) for piece in spread))  81.9 us
    pad x140, local copies, waits for them, and re-layouts, recurrent(): lax.associative_scan(combine_steps, (decay, (1.0 - rates) * values_in), a...  60.3 us
    slice x180, local copies, waits for them, and re-layouts, recurrent(): lax.associative_scan(combine_steps, (decay, (1.0 - rates) * values_in), a...  53.8 us
    all_gather x4, waiting for transfers between devices, layer_backward(): lax.all_gather(normed_rows, 'tensor', axis=0, tiled=True)  42.1 us
  transfers between devices with their start and end apart: 24, of which 11 were waited for; matrix products, arithmetic and copies ran while one was open for 40% of the time, Pallas kernels for 0%

commit v1 on v0

v1 whole, which is shorter than its diff:
```python
import functools

import jax
import jax.numpy as jnp
from jax import lax
from jax.experimental import pallas as pl
from jax.experimental.pallas import tpu as pltpu
from jax.sharding import PartitionSpec as P

EPSILON = 1e-05
XN = 4
YN = 4
MESH = pl.DeviceIdType.MESH
F32 = jnp.float32
BF16 = jnp.bfloat16
HIGHEST = lax.Precision.HIGHEST

AG_SEMS = 24
RS_SEMS = 32


def kernel(
    sections, x_down, x_up, g_down, g_up, loss_grad, w_in, w_out, gain, retention, layer_kind,
    out_down, out_up, out_in, out_out,
    mirror_x, mirror_g, xs, gs, gat, gps, csend, crecv, part, xrelay, xfrom, yacc, yrelay, yfrom,
    hop_send, hop_recv, back_send, back_recv, send_sem, recv_sem,
):
    half = w_in.shape[0] // 2
    s = lax.axis_index("section")
    t = lax.axis_index("tensor")
    core = lax.rem(t, 2)
    y = lax.rem(t // 2, YN)
    x = t // (2 * YN)
    xr, xl, xo = lax.rem(x + 1, XN), lax.rem(x + 3, XN), lax.rem(x + 2, XN)
    yr, yl, yo = lax.rem(y + 1, YN), lax.rem(y + 3, YN), lax.rem(y + 2, YN)

    def tensor_id(xx, yy, cc):
        return (xx * YN + yy) * 2 + cc

    to_xr = (s, tensor_id(xr, y, core))
    to_xl = (s, tensor_id(xl, y, core))
    to_yr = (s, tensor_id(x, yr, core))
    to_yl = (s, tensor_id(x, yl, core))
    to_core = (s, tensor_id(x, y, 1 - core))
    to_mirror = (sections - 1 - s, t)
    to_next = (lax.rem(s + sections - 1, sections), t)
    to_prev = (lax.rem(s + 1, sections), t)

    barrier = pltpu.get_barrier_semaphore()
    peers = (to_xr, to_xl, to_yr, to_yl, to_core, to_mirror, to_next, to_prev)
    for peer in peers:
        pl.semaphore_signal(barrier, inc=1, device_id=peer, device_id_type=MESH)
    pl.semaphore_wait(barrier, len(peers))

    sent = []
    count = [0]

    def send(src, dst, device):
        index = count[0]
        count[0] += 1
        copy = pltpu.make_async_remote_copy(
            src_ref=src, dst_ref=dst, send_sem=send_sem.at[index], recv_sem=recv_sem.at[index],
            device_id=device, device_id_type=MESH,
        )
        copy.start()
        sent.append(copy)
        return copy

    mx = send(x_up, mirror_x, to_mirror)
    mg = send(g_up, mirror_g, to_mirror)

    gain_f = gain[...].astype(F32)
    rates = retention[...].astype(F32)
    lane_kind = lax.broadcasted_iota(jnp.int32, layer_kind.shape, 1)
    kind = jnp.sum(jnp.where(lane_kind == s, layer_kind[...], 0), axis=1, keepdims=True)
    is_attention = kind == 1

    def recip_of(rows):
        return lax.rsqrt(jnp.mean(rows * rows, axis=-1, keepdims=True) + EPSILON)

    def put_unit(index, rows):
        for h in range(2):
            gat[index, h, core, x, y] = rows[:, h * half:(h + 1) * half]

    for tick in range(2):
        xs[tick, 0:4, :] = x_down[tick].astype(F32)
    gs[0, 0:4, :] = g_down[...].astype(F32)
    mx.wait_recv()
    for tick in range(2):
        xs[tick, 4:8, :] = mirror_x[tick].astype(F32)
    mg.wait_recv()
    gs[0, 4:8, :] = mirror_g[...].astype(F32)
    put_unit(1, gs[0].astype(BF16))
    for tick in range(2):
        rows = xs[tick]
        put_unit(2 * tick, (rows * recip_of(rows) * gain_f).astype(BF16))

    def gather(first, number):
        sets = pl.ds(first, number)

        def unit(xx, yy, h=None):
            if h is None:
                return gat.at[sets, :, core, xx, yy]
            return gat.at[sets, h, core, xx, yy]

        def both(xx, yy):
            ref = unit(xx, yy)
            return send(ref, ref, to_xr), send(ref, ref, to_xl)

        def across(xx):
            ref = gat.at[sets, :, core, xx]
            return send(ref, ref, to_core)

        own = unit(x, y)
        from_yl, from_yr = send(own, own, to_yr), send(own, own, to_yl)
        x_sends = [both(x, y)]
        yield
        from_yl.wait_recv()
        ref = unit(x, yl, 0)
        relay_r = send(ref, ref, to_yr)
        from_yr.wait_recv()
        ref = unit(x, yr, 1)
        relay_l = send(ref, ref, to_yl)
        x_sends.append(both(x, yl))
        x_sends.append(both(x, yr))
        yield
        relays = []

        def relay_x(k, yy):
            from_xl, from_xr = x_sends[k]
            from_xl.wait_recv()
            ref = unit(xl, yy, 0)
            right = send(ref, ref, to_xr)
            from_xr.wait_recv()
            ref = unit(xr, yy, 1)
            relays.append((right, send(ref, ref, to_xl)))

        relay_x(0, y)
        relay_r.wait_recv()
        relay_l.wait_recv()
        x_sends.append(both(x, yo))
        crossing = [across(x)]
        yield
        relay_x(1, yl)
        relay_x(2, yr)
        yield
        relay_x(3, yo)
        crossing.append(across(xl))
        crossing.append(across(xr))
        yield
        for right, left in relays:
            right.wait_recv()
            left.wait_recv()
        crossing.append(across(xo))
        yield
        for copy in crossing:
            copy.wait_recv()

    def finish(steps):
        for _ in steps:
            pass

    def gathered(index, h):
        return gat[index, h].reshape(256, half)

    upper = lax.rem(lax.broadcasted_iota(jnp.int32, (128, 128), 0), 8) < 4

    def to_tokens(rows):
        first, second = rows[:128], rows[128:]
        down = jnp.where(upper, first, pltpu.roll(second, 4, 0))
        up = jnp.where(upper, pltpu.roll(first, 124, 0), second)
        return down, up

    def to_gathered(down, up):
        first = jnp.where(upper, down, pltpu.roll(up, 4, 0))
        second = jnp.where(upper, pltpu.roll(down, 124, 0), up)
        return first, second

    def projected_of(index):
        total = jnp.dot(gathered(index, 0), w_in[:half, :], preferred_element_type=F32)
        return total + jnp.dot(gathered(index, 1), w_in[half:, :], preferred_element_type=F32)

    def contract_last(left, right, **kw):
        return lax.dot_general(left, right, (((1,), (1,)), ((), ())), preferred_element_type=F32, **kw)

    def contract_first(left, right, **kw):
        return lax.dot_general(left, right, (((0,), (0,)), ((), ())), preferred_element_type=F32, **kw)

    def grad_mixed_of(index):
        total = contract_last(gathered(index, 0), w_out[:, :half])
        return total + contract_last(gathered(index, 1), w_out[:, half:])

    token = lax.broadcasted_iota(jnp.int32, (128, 256), 0)
    causal = lax.broadcasted_iota(jnp.int32, (128, 128), 0) >= lax.broadcasted_iota(jnp.int32, (128, 128), 1)
    low_lane = lax.broadcasted_iota(jnp.int32, (128, 128), 1) < 64
    rates2 = jnp.concatenate([rates, rates], axis=1)

    def scan(values, backward):
        state = values
        power = rates2
        step = 1
        while step < 128:
            if backward:
                moved = jnp.where(token < 128 - step, pltpu.roll(state, 128 - step, 0), 0.0)
            else:
                moved = jnp.where(token >= step, pltpu.roll(state, step, 0), 0.0)
            state = state + power * moved
            power = power * power
            step *= 2
        return state

    def mix_forward(pair):
        wide = jnp.concatenate(pair, axis=1)
        state = scan((1.0 - rates2) * wide, False)
        gate = jax.nn.sigmoid(wide)
        recurrent = state * (wide * gate)
        weights, mixed = [], []
        for d in range(2):
            v = pair[d]
            turned = pltpu.roll(v, 64, 1)
            scores = contract_last(jnp.where(low_lane, v, 0.0), turned, precision=HIGHEST) * 0.125
            scores = jnp.where(causal, scores, -1e30)
            w = jnp.exp(scores - jnp.max(scores, axis=-1, keepdims=True))
            w = w / jnp.sum(w, axis=-1, keepdims=True)
            attended = jnp.dot(w, v, precision=HIGHEST, preferred_element_type=F32)
            weights.append(w)
            mixed.append(jnp.where(is_attention, attended, recurrent[:, d * 128:(d + 1) * 128]))
        return mixed, (pair, wide, state, gate, weights)

    def mix_backward(saved, grads):
        pair, wide, state, gate, weights = saved
        g_wide = jnp.concatenate(grads, axis=1)
        d_state = scan(g_wide * (wide * gate), True)
        recurrent = (1.0 - rates2) * d_state + g_wide * state * (gate * (1.0 + wide * (1.0 - gate)))
        result = []
        for d in range(2):
            v, g, w = pair[d], grads[d], weights[d]
            turned = pltpu.roll(v, 64, 1)
            d_weights = contract_last(g, v, precision=HIGHEST)
            d_scores = w * (d_weights - jnp.sum(w * d_weights, axis=-1, keepdims=True)) * 0.125
            d_query = jnp.dot(d_scores, turned, precision=HIGHEST, preferred_element_type=F32)
            d_key = contract_first(d_scores, v, precision=HIGHEST)
            attended = contract_first(w, g, precision=HIGHEST) + jnp.where(
                low_lane, d_query, pltpu.roll(d_key, 64, 1)
            )
            result.append(jnp.where(is_attention, attended, recurrent[:, d * 128:(d + 1) * 128]))
        return result

    y_order = (yo, yr, yl, y)

    def add(*pieces):
        total = pieces[0].astype(F32)
        for piece in pieces[1:]:
            total = total + piece.astype(F32)
        return total

    def scatter(tick):
        def terms(which, h):
            weights = w_in[h * half:(h + 1) * half, :]
            return contract_last(gps[tick, which], weights).astype(BF16).reshape(XN, YN, 8, half)

        crossing = []
        for h in range(2):
            csend[tick, h] = terms(1 - core, h)
            crossing.append(send(csend.at[tick, h], crecv.at[tick, h], to_core))
        yield
        for h in range(2):
            own = terms(core, h)
            crossing[h].wait_recv()
            part[tick, h] = add(own, crecv[tick, h]).astype(BF16)
        first, plain, joined = [], [], []
        p, xy, xf = part.at[tick], xrelay.at[tick], xfrom.at[tick]
        for yy in y_order:
            first.append((
                send(p.at[0, xo, yy], xy.at[0, yy], to_xr),
                send(p.at[1, xo, yy], xy.at[1, yy], to_xl),
            ))
        for yy in y_order:
            plain.append((
                send(p.at[1, xr, yy], xf.at[0, 1, yy], to_xr),
                send(p.at[0, xl, yy], xf.at[1, 0, yy], to_xl),
            ))
        yield
        for k, yy in enumerate(y_order):
            first[k][0].wait_recv()
            part[tick, 0, xr, yy] = add(part[tick, 0, xr, yy], xrelay[tick, 0, yy]).astype(BF16)
            right = send(p.at[0, xr, yy], xf.at[0, 0, yy], to_xr)
            first[k][1].wait_recv()
            part[tick, 1, xl, yy] = add(part[tick, 1, xl, yy], xrelay[tick, 1, yy]).astype(BF16)
            joined.append((right, send(p.at[1, xl, yy], xf.at[1, 1, yy], to_xl)))
            if k % 2 == 1:
                yield

        def reduce_x(k):
            yy = y_order[k]
            for copy in plain[k] + joined[k]:
                copy.wait_recv()
            for h in range(2):
                yacc[tick, h, yy] = add(
                    part[tick, h, x, yy], xfrom[tick, 0, h, yy], xfrom[tick, 1, h, yy]
                ).astype(BF16)

        q, yrl, yf = yacc.at[tick], yrelay.at[tick], yfrom.at[tick]
        reduce_x(0)
        first_r = send(q.at[0, yo], yrl.at[0], to_yr)
        first_l = send(q.at[1, yo], yrl.at[1], to_yl)
        reduce_x(1)
        plain_r = send(q.at[1, yr], yf.at[0, 1], to_yr)
        reduce_x(2)
        plain_l = send(q.at[0, yl], yf.at[1, 0], to_yl)
        yield
        first_r.wait_recv()
        yacc[tick, 0, yr] = add(yacc[tick, 0, yr], yrelay[tick, 0]).astype(BF16)
        joined_r = send(q.at[0, yr], yf.at[0, 0], to_yr)
        first_l.wait_recv()
        yacc[tick, 1, yl] = add(yacc[tick, 1, yl], yrelay[tick, 1]).astype(BF16)
        joined_l = send(q.at[1, yl], yf.at[1, 1], to_yl)
        yield
        reduce_x(3)
        for copy in (plain_r, plain_l, joined_r, joined_l):
            copy.wait_recv()
        halves = [
            add(yacc[tick, h, y], yfrom[tick, 0, h], yfrom[tick, 1, h]) for h in range(2)
        ]
        rows = xs[tick]
        recip = recip_of(rows)
        scaled = jnp.concatenate(halves, axis=1) * gain_f
        along = jnp.mean(scaled * rows, axis=-1, keepdims=True)
        xs[tick] = gs[tick] + (recip * scaled - rows * (recip * recip * recip) * along)

    gather_1 = gather(0, 2)
    for _ in range(6):
        next(gather_1)
    gather_2 = gather(2, 1)
    next(gather_2)
    finish(gather_1)

    def split_rows(pair):
        first, second = to_gathered(*pair)
        return first, second

    def spread(first, second):
        rows = jnp.concatenate([first, second], axis=0)
        mask = lax.rem(lax.broadcasted_iota(jnp.int32, (256, 128), 0), 8) < 4
        return jnp.concatenate([jnp.where(mask, rows, 0.0), jnp.where(mask, 0.0, rows)], axis=1)

    pair_1 = to_tokens(projected_of(0))
    grads_1 = to_tokens(grad_mixed_of(1))
    next(gather_2)
    mixed_1, saved_1 = mix_forward(pair_1)
    d_pair = mix_backward(saved_1, grads_1)
    next(gather_2)
    first, second = split_rows(d_pair)
    gps[0, 0] = first.astype(BF16)
    gps[0, 1] = second.astype(BF16)
    gp_wide_1 = spread(first, second).astype(BF16)
    mixed_wide_1 = spread(*split_rows(mixed_1)).astype(BF16)
    scatter_1 = scatter(0)
    next(scatter_1)
    next(gather_2)
    next(scatter_1)
    next(gather_2)
    next(scatter_1)
    next(gather_2)
    next(scatter_1)
    finish(gather_2)
    pair_2 = to_tokens(projected_of(2))
    next(scatter_1)
    next(scatter_1)
    finish(scatter_1)
    hop_send[...] = xs[0].astype(BF16)
    hop = send(hop_send, hop_recv, to_next)
    mixed_2, saved_2 = mix_forward(pair_2)
    mixed_wide_2 = spread(*split_rows(mixed_2)).astype(BF16)
    hop.wait_recv()
    gs[1, 0:4, :] = loss_grad[0].astype(F32)
    gs[1, 4:8, :] = loss_grad[1].astype(F32)
    gs[1] = jnp.where(s == sections - 1, gs[1], hop_recv[...].astype(F32))
    put_unit(3, gs[1].astype(BF16))
    finish(gather(3, 1))
    grads_2 = to_tokens(grad_mixed_of(3))
    first, second = split_rows(mix_backward(saved_2, grads_2))
    gps[1, 0] = first.astype(BF16)
    gps[1, 1] = second.astype(BF16)
    gp_wide_2 = spread(first, second).astype(BF16)
    scatter_2 = scatter(1)
    next(scatter_2)
    next(scatter_2)

    block = 256
    per_half = half // block
    gp_both = jnp.concatenate([gp_wide_1, gp_wide_2], axis=0)
    mixed_both = jnp.concatenate([mixed_wide_1, mixed_wide_2], axis=0)

    def columns(index, h, at):
        return gat[index, h, :, :, :, :, pl.ds(at, block)].reshape(256, block)

    def weight_in(h):
        def step(i, _):
            at = pl.multiple_of(i * block, block)
            left = jnp.concatenate([columns(0, h, at), columns(2, h, at)], axis=0)
            total = contract_first(left, gp_both)
            down = total[:, :128].astype(BF16).astype(F32)
            up = total[:, 128:].astype(BF16).astype(F32)
            out_in[pl.ds(h * half + at, block), :] = (down + up).astype(BF16)
            return 0

        lax.fori_loop(0, per_half, step, 0)

    def weight_out(h):
        def step(i, _):
            at = pl.multiple_of(i * block, block)
            right = jnp.concatenate([columns(1, h, at), columns(3, h, at)], axis=0)
            total = contract_first(mixed_both, right)
            down = total[:128].astype(BF16).astype(F32)
            up = total[128:].astype(BF16).astype(F32)
            out_out[:, pl.ds(h * half + at, block)] = (down + up).astype(BF16)
            return 0

        lax.fori_loop(0, per_half, step, 0)

    weight_out(0)
    next(scatter_2)
    weight_out(1)
    next(scatter_2)
    weight_in(0)
    next(scatter_2)
    next(scatter_2)
    finish(scatter_2)
    back_send[...] = xs[1, 4:8, :].astype(BF16)
    back = send(back_send, back_recv, to_mirror)
    out_down[...] = xs[1, 0:4, :].astype(BF16)
    weight_in(1)
    back.wait_recv()
    out_up[...] = back_recv[...]
    for copy in sent:
        copy.wait_send()


def body(x_down, x_up, g_down, g_up, loss_grad, w_in, w_out, gain, retention, layer_kind):
    sections = lax.axis_size("section")
    width = w_in.shape[1]
    half = width // 2
    vmem = pl.BlockSpec(memory_space=pltpu.VMEM)
    copies = 3 * AG_SEMS + 2 * RS_SEMS + 4
    down, up, grad_in, grad_out = pl.pallas_call(
        functools.partial(kernel, sections),
        out_shape=(
            jax.ShapeDtypeStruct((4, width), BF16),
            jax.ShapeDtypeStruct((4, width), BF16),
            jax.ShapeDtypeStruct((width, 128), BF16),
            jax.ShapeDtypeStruct((128, width), BF16),
        ),
        in_specs=[vmem] * 10,
        out_specs=(vmem,) * 4,
        scratch_shapes=[
            pltpu.VMEM((2, 4, width), BF16),
            pltpu.VMEM((4, width), BF16),
            pltpu.VMEM((2, 8, width), F32),
            pltpu.VMEM((2, 8, width), F32),
            pltpu.VMEM((4, 2, 2, XN, YN, 8, half), BF16),
            pltpu.VMEM((2, 2, 128, 128), BF16),
            pltpu.VMEM((2, 2, XN, YN, 8, half), BF16),
            pltpu.VMEM((2, 2, XN, YN, 8, half), BF16),
            pltpu.VMEM((2, 2, XN, YN, 8, half), BF16),
            pltpu.VMEM((2, 2, YN, 8, half), BF16),
            pltpu.VMEM((2, 2, 2, YN, 8, half), BF16),
            pltpu.VMEM((2, 2, YN, 8, half), BF16),
            pltpu.VMEM((2, 2, 8, half), BF16),
            pltpu.VMEM((2, 2, 2, 8, half), BF16),
            pltpu.VMEM((8, width), BF16),
            pltpu.VMEM((8, width), BF16),
            pltpu.VMEM((4, width), BF16),
            pltpu.VMEM((4, width), BF16),
            pltpu.SemaphoreType.DMA((copies,)),
            pltpu.SemaphoreType.DMA((copies,)),
        ],
        compiler_params=pltpu.CompilerParams(
            collective_id=0, has_side_effects=True, vmem_limit_bytes=56 * 1024 * 1024
        ),
    )(
        x_down[:, 0], x_up[:, 0], g_down[0], g_up[0], loss_grad, w_in[0], w_out[0], gain, retention,
        layer_kind.reshape(1, -1),
    )
    return (down[None], up[None], grad_in[None], grad_out[None])


def solution(mesh):
    return jax.shard_map(
        body,
        mesh=mesh,
        in_specs=(
            P(None, "section", "tensor", None),
            P(None, "section", "tensor", None),
            P("section", "tensor", None),
            P("section", "tensor", None),
            P(None, "tensor", None),
            P("section", None, "tensor"),
            P("section", "tensor", None),
            P("section", None),
            P("section", "tensor"),
            P(),
        ),
        out_specs=(
            P("section", "tensor", None),
            P("section", "tensor", None),
            P("section", None, "tensor"),
            P("section", "tensor", None),
        ),
        check_vma=False,
    )
```

time: 1540 us -> 137 us (0.09)
  the two profiles are of different devices: /device:TPU:1 before, /device:TPU:24 now
where the time goes in v1:
time: 137 us
  Pallas kernels  131 us (96%)
  local copies, waits for them, and re-layouts  5.33 us (4%)
    pallas_call x1, Pallas kernels, body(): pl.pallas_call(functools.partial(kernel, sections), out_shape=(jax.ShapeD...  131 us
    unnamed x8, local copies, waits for them, and re-layouts  5.33 us

profile of v1, /device:TPU:24, one launch (start us, length us, event | category | flops | bytes accessed | tf_op | source)
XLA Modules:
  0.0 136.9 jit_solution(2103783778296689671)
XLA Ops:
  0.6 130.9 %shard_map.129 = (bf16[4,4096]{1,0:T(4,128)(2,1)}, bf16[4,4096]{1,0:T(4,128)(2,1)}, bf16[4096,128]{1,0:T(8,128)(2,1)}, bf16[128,4096]{1,0:T(8,128)(2,1)}) custom-call(bf16[2,4,4096]{2,1,0:T(4,128)(2,1)} %bitcast.15, bf16[2,4,4096]{2,1,0:T(4,128)(2,1)} %bitcast.16, bf16[4,4096]{1,0:T(4,128)(2,1)} %bitcast.17, bf16[4,4096]{1,0:T(4,128)(2,1)} %bitcast.18, ...), custom_call_target="tpu_custom_call" | custom-call | tf_op jit(solution)/shard_map/pallas_call | solution.py:446
  131.6 0.0 copy-start.1
  131.6 1.4 %copy.18 = bf16[1,4,4096]{2,1,0:T(4,128)(2,1)} copy(bf16[1,4,4096]{2,1,0:T(4,128)(2,1)} %bitcast.20) | data formatting | bytes 65536
  133.0 0.0 copy-done.1
  133.0 0.6 copy.19
  133.6 0.0 copy-start
  133.6 2.4 %copy.20 = bf16[1,4096,128]{2,1,0:T(8,128)(2,1)} copy(bf16[1,4096,128]{2,1,0:T(8,128)(2,1)} %bitcast.14) | data formatting | bytes 2097152
  135.9 0.0 copy-done
  135.9 1.0 copy.21
Async XLA Ops:
  131.6 1.4 %copy-start.1 = (bf16[4,4096]{1,0:T(4,128)(2,1)S(1)}, bf16[4,4096]{1,0:T(4,128)(2,1)}, u32[]{:S(2)}) copy-start(bf16[4,4096]{1,0:T(4,128)(2,1)} %get-tuple-element.9) | copy-start | bytes 98308
  133.6 2.4 %copy-start = (bf16[128,4096]{1,0:T(8,128)(2,1)S(1)}, bf16[128,4096]{1,0:T(8,128)(2,1)}, u32[]{:S(2)}) copy-start(bf16[128,4096]{1,0:T(8,128)(2,1)} %get-tuple-element.11) | copy-start | bytes 3145732

commit v2 on v0

v2 whole, which is shorter than its diff:
```python
import functools

import jax
import jax.numpy as jnp
from jax import lax
from jax.experimental import pallas as pl
from jax.experimental.pallas import tpu as pltpu
from jax.sharding import PartitionSpec as P

EPSILON = 1e-05
XN = 4
YN = 4
Y_DIRECT = False
X_DIRECT = False
SHARED_AT = 3
MESH = pl.DeviceIdType.MESH
F32 = jnp.float32
BF16 = jnp.bfloat16
HIGHEST = lax.Precision.HIGHEST

AG_SEMS = 24
RS_SEMS = 32


def kernel(
    sections, x_down_h, x_up_h, g_down_h, g_up_h, loss_h, w_in_h, w_out_h, gain_h, retention_h, kind_h,
    down_h, up_h, in_h, out_h,
    x_rows, g_rows, loss_rows, w_in, w_out, gain, retention, layer_kind, out_down, back_send, back_recv,
    out_in, out_out, load_sem, store_sem,
    xs, gs, gat, csend, crecv, part, xrelay, xfrom, yacc, yrelay, yfrom,
    pre_send, pre_recv, fin_send, fin_recv, hop_send, hop_recv, side_send, side_recv,
    send_sem, recv_sem,
):
    width = w_in.shape[0]
    half = width // 2
    quarter = width // 4
    loads = [
        pltpu.make_async_copy(src, dst, load_sem.at[i])
        for i, (src, dst) in enumerate((
            (x_down_h, x_rows.at[0]), (g_down_h, g_rows.at[0]), (gain_h, gain), (loss_h, loss_rows),
            (retention_h, retention), (kind_h, layer_kind), (w_in_h, w_in), (w_out_h, w_out),
        ))
    ]
    for copy in loads:
        copy.start()
    s = lax.axis_index("section")
    t = lax.axis_index("tensor")
    core = lax.rem(t, 2)
    y = lax.rem(t // 2, YN)
    x = t // (2 * YN)
    xr, xl, xo = lax.rem(x + 1, XN), lax.rem(x + 3, XN), lax.rem(x + 2, XN)
    yr, yl, yo = lax.rem(y + 1, YN), lax.rem(y + 3, YN), lax.rem(y + 2, YN)

    def tensor_id(xx, yy, cc):
        return (xx * YN + yy) * 2 + cc

    next_section = lax.rem(s + sections - 1, sections)
    prev_section = lax.rem(s + 1, sections)
    other = tensor_id(x, y, 1 - core)
    to_xr = (s, tensor_id(xr, y, core))
    to_xl = (s, tensor_id(xl, y, core))
    to_yr = (s, tensor_id(x, yr, core))
    to_yl = (s, tensor_id(x, yl, core))
    to_xo = (s, tensor_id(xo, y, core))
    to_yo = (s, tensor_id(x, yo, core))
    to_core = (s, other)
    to_mirror = (sections - 1 - s, t)
    to_next, to_next_side = (next_section, t), (next_section, other)
    to_prev, to_prev_side = (prev_section, t), (prev_section, other)

    barrier = pltpu.get_barrier_semaphore()
    peers = [
        to_xr, to_xl, to_yr, to_yl, to_core, to_mirror, to_next, to_prev, to_next_side, to_prev_side,
    ]
    if Y_DIRECT:
        peers.append(to_yo)
    if X_DIRECT:
        peers.append(to_xo)
    for peer in peers:
        pl.semaphore_signal(barrier, inc=1, device_id=peer, device_id_type=MESH)
    pl.semaphore_wait(barrier, len(peers))

    sent = []

    def send(src, dst, device):
        index = len(sent)
        copy = pltpu.make_async_remote_copy(
            src_ref=src, dst_ref=dst, send_sem=send_sem.at[index], recv_sem=recv_sem.at[index],
            device_id=device, device_id_type=MESH,
        )
        copy.start()
        sent.append(copy)
        return copy

    stores = []

    def store(src, dst):
        copy = pltpu.make_async_copy(src, dst, store_sem.at[len(stores)])
        copy.start()
        stores.append(copy)

    mx = send(x_up_h, x_rows.at[1], to_mirror)
    mg = send(g_up_h, g_rows.at[1], to_mirror)
    for copy in loads[:6]:
        copy.wait()

    gain_f = gain[...].astype(F32)
    rates = retention[...].astype(F32)
    lane_kind = lax.broadcasted_iota(jnp.int32, layer_kind.shape, 1)
    kind = jnp.sum(jnp.where(lane_kind == s, layer_kind[...], 0), axis=1, keepdims=True)
    is_attention = kind == 1
    first_core = core == 0

    def recip_of(rows):
        return lax.rsqrt(jnp.mean(rows * rows, axis=-1, keepdims=True) + EPSILON)

    def mine(rows):
        return jnp.where(first_core, rows[:, :half], rows[:, half:])

    def theirs(rows):
        return jnp.where(first_core, rows[:, half:], rows[:, :half])

    def put_unit(d, index, own, received):
        first = jnp.where(first_core, own, received)
        second = jnp.where(first_core, received, own)
        unit = jnp.concatenate([first, second], axis=0).astype(BF16)
        for q in range(2):
            gat[d, index, core, q, x, y] = unit[:, q * quarter:(q + 1) * quarter]

    def prepare(d):
        kept = []
        for tick in range(2):
            rows = x_rows[d, tick].astype(F32)
            xs[d, tick] = rows
            normed = (rows * recip_of(rows) * gain_f).astype(BF16).astype(F32)
            pre_send[d, 2 * tick] = theirs(normed).astype(BF16)
            kept.append(mine(normed))
        grads = g_rows[d].astype(F32)
        gs[d, 0] = grads
        pre_send[d, 1] = theirs(grads).astype(BF16)
        pre_send[d, 3] = theirs(loss_rows[d].astype(F32)).astype(BF16)
        copy = send(pre_send.at[d], pre_recv.at[d], to_core)
        copy.wait_recv()
        put_unit(d, 0, kept[0], pre_recv[d, 0].astype(F32))
        put_unit(d, 1, mine(grads), pre_recv[d, 1].astype(F32))
        put_unit(d, 2, kept[1], pre_recv[d, 2].astype(F32))

    def gather(directions, sets):
        def unit(xx, yy, q=None):
            if q is None:
                return gat.at[directions, sets, core, :, xx, yy]
            return gat.at[directions, sets, core, q, xx, yy]

        def spread_x(yy):
            ref = unit(x, yy)
            copies = [send(ref, ref, to_xr), send(ref, ref, to_xl)]
            if X_DIRECT:
                copies.append(send(ref, ref, to_xo))
            return copies

        def across(xx):
            ref = gat.at[directions, sets, core, :, xx]
            return send(ref, ref, to_core)

        own = unit(x, y)
        from_yl, from_yr = send(own, own, to_yr), send(own, own, to_yl)
        if Y_DIRECT:
            from_yo = [send(own, own, to_yo)]
        x_sends = [spread_x(y)]
        yield
        from_yl.wait_recv()
        if not Y_DIRECT:
            ref = unit(x, yl, 0)
            from_yo = [send(ref, ref, to_yr)]
        x_sends.append(spread_x(yl))
        from_yr.wait_recv()
        if not Y_DIRECT:
            ref = unit(x, yr, 1)
            from_yo.append(send(ref, ref, to_yl))
        x_sends.append(spread_x(yr))
        yield
        relays = []

        def relay_x(k, yy):
            x_sends[k][0].wait_recv()
            if not X_DIRECT:
                ref = unit(xl, yy, 0)
                relays.append(send(ref, ref, to_xr))
            x_sends[k][1].wait_recv()
            if not X_DIRECT:
                ref = unit(xr, yy, 1)
                relays.append(send(ref, ref, to_xl))

        if not Y_DIRECT:
            relay_x(0, y)
        for copy in from_yo:
            copy.wait_recv()
        x_sends.append(spread_x(yo))
        if Y_DIRECT:
            relay_x(0, y)
        crossing = [across(x)]
        yield
        relay_x(1, yl)
        relay_x(2, yr)
        yield
        relay_x(3, yo)
        crossing.append(across(xl))
        crossing.append(across(xr))
        yield
        for copy in relays:
            copy.wait_recv()
        if X_DIRECT:
            for copies in x_sends:
                copies[2].wait_recv()
        crossing.append(across(xo))
        yield
        for copy in crossing:
            copy.wait_recv()

    def gathered(d, index, i):
        return gat[d, index, i // 2, i % 2].reshape(128, quarter)

    def contract_last(left, right, **kw):
        return lax.dot_general(left, right, (((1,), (1,)), ((), ())), preferred_element_type=F32, **kw)

    def contract_first(left, right, **kw):
        return lax.dot_general(left, right, (((0,), (0,)), ((), ())), preferred_element_type=F32, **kw)

    def projected_of(d, index):
        total = 0.0
        for i in range(4):
            total = total + jnp.dot(
                gathered(d, index, i), w_in[i * quarter:(i + 1) * quarter, :], preferred_element_type=F32
            )
        return total

    def grad_mixed_of(d, index):
        total = 0.0
        for i in range(4):
            total = total + contract_last(gathered(d, index, i), w_out[:, i * quarter:(i + 1) * quarter])
        return total

    token = lax.broadcasted_iota(jnp.int32, (128, 128), 0)
    lane = lax.broadcasted_iota(jnp.int32, (128, 128), 1)
    causal = token >= lane
    low_lane = lane < 64

    def scan(values, backward):
        state = values
        power = rates
        step = 1
        while step < 128:
            if backward:
                moved = jnp.where(token < 128 - step, pltpu.roll(state, 128 - step, 0), 0.0)
            else:
                moved = jnp.where(token >= step, pltpu.roll(state, step, 0), 0.0)
            state = state + power * moved
            power = power * power
            step *= 2
        return state

    def mix_forward(v):
        state = scan((1.0 - rates) * v, False)
        gate = jax.nn.sigmoid(v)
        recurrent = state * (v * gate)
        turned = pltpu.roll(v, 64, 1)
        scores = contract_last(jnp.where(low_lane, v, 0.0), turned, precision=HIGHEST) * 0.125
        scores = jnp.where(causal, scores, -1e30)
        weights = jnp.exp(scores - jnp.max(scores, axis=-1, keepdims=True))
        weights = weights / jnp.sum(weights, axis=-1, keepdims=True)
        attended = jnp.dot(weights, v, precision=HIGHEST, preferred_element_type=F32)
        mixed = jnp.where(is_attention, attended, recurrent)
        return mixed.astype(BF16), (v, state, gate, weights)

    def mix_backward(saved, g):
        v, state, gate, weights = saved
        d_state = scan(g * (v * gate), True)
        recurrent = (1.0 - rates) * d_state + g * state * (gate * (1.0 + v * (1.0 - gate)))
        turned = pltpu.roll(v, 64, 1)
        d_weights = contract_last(g, v, precision=HIGHEST)
        d_scores = weights * (d_weights - jnp.sum(weights * d_weights, axis=-1, keepdims=True)) * 0.125
        d_query = jnp.dot(d_scores, turned, precision=HIGHEST, preferred_element_type=F32)
        d_key = contract_first(d_scores, v, precision=HIGHEST)
        attended = contract_first(weights, g, precision=HIGHEST) + jnp.where(
            low_lane, d_query, pltpu.roll(d_key, 64, 1)
        )
        return jnp.where(is_attention, attended, recurrent).astype(BF16)

    y_order = (yo, yr, yl, y)

    def add(*pieces):
        total = pieces[0].astype(F32)
        for piece in pieces[1:]:
            total = total + piece.astype(F32)
        return total

    def scatter(d, tick, grad_proj):
        def terms(which, q):
            at = pl.multiple_of(which * half + q * quarter, quarter)
            weights = w_in[pl.ds(at, quarter), :]
            return contract_last(grad_proj, weights).astype(BF16).reshape(XN, YN, 8, quarter)

        crossing = []
        for q in range(2):
            csend[d, tick, q] = terms(1 - core, q)
            crossing.append(send(csend.at[d, tick, q], crecv.at[d, tick, q], to_core))
        own = [terms(core, q) for q in range(2)]
        yield
        for q in range(2):
            crossing[q].wait_recv()
            part[d, tick, q] = add(own[q], crecv[d, tick, q]).astype(BF16)
        first, plain, joined = [], [], []
        p, xy, xf = part.at[d, tick], xrelay.at[d, tick], xfrom.at[d, tick]
        if X_DIRECT:
            for yy in y_order:
                plain.append([
                    send(p.at[:, xo, yy], xf.at[2, :, yy], to_xo),
                    send(p.at[:, xr, yy], xf.at[0, :, yy], to_xr),
                    send(p.at[:, xl, yy], xf.at[1, :, yy], to_xl),
                ])
                joined.append([])
            yield
        else:
            for yy in y_order:
                first.append((
                    send(p.at[0, xo, yy], xy.at[0, yy], to_xr),
                    send(p.at[1, xo, yy], xy.at[1, yy], to_xl),
                ))
                plain.append([
                    send(p.at[1, xr, yy], xf.at[0, 1, yy], to_xr),
                    send(p.at[0, xl, yy], xf.at[1, 0, yy], to_xl),
                ])
            yield
            for k, yy in enumerate(y_order):
                first[k][0].wait_recv()
                part[d, tick, 0, xr, yy] = add(part[d, tick, 0, xr, yy], xrelay[d, tick, 0, yy]).astype(BF16)
                right = send(p.at[0, xr, yy], xf.at[0, 0, yy], to_xr)
                first[k][1].wait_recv()
                part[d, tick, 1, xl, yy] = add(part[d, tick, 1, xl, yy], xrelay[d, tick, 1, yy]).astype(BF16)
                joined.append([right, send(p.at[1, xl, yy], xf.at[1, 1, yy], to_xl)])
                if k % 2 == 1:
                    yield

        def reduce_x(k):
            yy = y_order[k]
            for copy in plain[k] + joined[k]:
                copy.wait_recv()
            for q in range(2):
                pieces = [xfrom[d, tick, i, q, yy] for i in range(3 if X_DIRECT else 2)]
                yacc[d, tick, q, yy] = add(part[d, tick, q, x, yy], *pieces).astype(BF16)

        a, yrl, yf = yacc.at[d, tick], yrelay.at[d, tick], yfrom.at[d, tick]
        reduce_x(0)
        if Y_DIRECT:
            last = [send(a.at[:, yo], yf.at[2], to_yo)]
            reduce_x(1)
            last.append(send(a.at[:, yr], yf.at[0], to_yr))
            reduce_x(2)
            last.append(send(a.at[:, yl], yf.at[1], to_yl))
            reduce_x(3)
            yield
        else:
            first_r = send(a.at[0, yo], yrl.at[0], to_yr)
            first_l = send(a.at[1, yo], yrl.at[1], to_yl)
            reduce_x(1)
            last = [send(a.at[1, yr], yf.at[0, 1], to_yr)]
            reduce_x(2)
            last.append(send(a.at[0, yl], yf.at[1, 0], to_yl))
            reduce_x(3)
            yield
            first_r.wait_recv()
            yacc[d, tick, 0, yr] = add(yacc[d, tick, 0, yr], yrelay[d, tick, 0]).astype(BF16)
            last.append(send(a.at[0, yr], yf.at[0, 0], to_yr))
            first_l.wait_recv()
            yacc[d, tick, 1, yl] = add(yacc[d, tick, 1, yl], yrelay[d, tick, 1]).astype(BF16)
            last.append(send(a.at[1, yl], yf.at[1, 1], to_yl))
            yield
        for copy in last:
            copy.wait_recv()
        summed = jnp.concatenate([
            add(yacc[d, tick, q, y], *[yfrom[d, tick, i, q] for i in range(3 if Y_DIRECT else 2)])
            for q in range(2)
        ], axis=1)
        fin_send[d, tick] = jnp.where(first_core, summed[4:], summed[:4])
        swap = send(fin_send.at[d, tick], fin_recv.at[d, tick], to_core)
        kept = jnp.where(first_core, summed[:4], summed[4:])
        rows = xs[d, tick]
        recip = recip_of(rows)
        swap.wait_recv()
        received = fin_recv[d, tick]
        scaled = jnp.concatenate([
            jnp.where(first_core, kept, received), jnp.where(first_core, received, kept)
        ], axis=1) * gain_f
        along = jnp.mean(scaled * rows, axis=-1, keepdims=True)
        xs[d, tick] = gs[d, tick] + (recip * scaled - rows * (recip * recip * recip) * along)

    block = min(256, quarter)
    per_quarter = quarter // block

    def columns(d, index, i, at):
        return gat[d, index, i // 2, i % 2, :, :, :, pl.ds(at, block)].reshape(128, block)

    def both_ticks(d, index, i, at):
        return jnp.concatenate([columns(d, index, i, at), columns(d, index + 2, i, at)], axis=0)

    def weight_in(d, i, grad_both):
        def step(j, _):
            at = pl.multiple_of(j * block, block)
            rows = pl.ds(i * quarter + at, block)
            total = contract_first(both_ticks(d, 0, i, at), grad_both).astype(BF16)
            if d == 1:
                total = (out_in[rows, :].astype(F32) + total.astype(F32)).astype(BF16)
            out_in[rows, :] = total
            return 0

        lax.fori_loop(0, per_quarter, step, 0)

    def weight_out(d, i, mixed_turned):
        def step(j, _):
            at = pl.multiple_of(j * block, block)
            cols = pl.ds(i * quarter + at, block)
            total = jnp.dot(mixed_turned, both_ticks(d, 1, i, at), preferred_element_type=F32).astype(BF16)
            if d == 1:
                total = (out_out[:, cols].astype(F32) + total.astype(F32)).astype(BF16)
            out_out[:, cols] = total
            return 0

        lax.fori_loop(0, per_quarter, step, 0)

    def chain(d):
        one = pl.ds(d, 1)
        yield from gather(one, pl.ds(0, 2))
        if d == 0:
            loads[6].wait()
            loads[7].wait()
        mixed_1, saved = mix_forward(projected_of(d, 0))
        grad_proj_1 = mix_backward(saved, grad_mixed_of(d, 1))
        yield from scatter(d, 0, grad_proj_1)
        hop_send[d] = xs[d, 0].astype(BF16)
        side_send[d] = theirs(xs[d, 0]).astype(BF16)
        hop = send(hop_send.at[d], hop_recv.at[d], to_next)
        side = send(side_send.at[d], side_recv.at[d], to_next_side)
        yield "second"
        mixed_2, saved = mix_forward(projected_of(d, 2))
        mixed_turned = jnp.concatenate(
            [mixed_1.astype(F32), mixed_2.astype(F32)], axis=0
        ).T.astype(BF16)
        hop.wait_recv()
        side.wait_recv()
        at_top = s == sections - 1
        grads = jnp.where(at_top, loss_rows[d].astype(F32), hop_recv[d].astype(F32))
        gs[d, 1] = grads
        put_unit(
            d, 3, mine(grads),
            jnp.where(at_top, pre_recv[d, 3].astype(F32), side_recv[d].astype(F32)),
        )
        yield from gather(one, pl.ds(3, 1))
        grad_proj_2 = mix_backward(saved, grad_mixed_of(d, 3))
        steps = scatter(d, 1, grad_proj_2)
        grad_both = jnp.concatenate([grad_proj_1, grad_proj_2], axis=0)
        work = [functools.partial(weight_out, d, i, mixed_turned) for i in range(4)]
        work += [functools.partial(weight_in, d, i, grad_both) for i in range(4)]
        for _ in steps:
            yield
            if work:
                work.pop(0)()
        if d == 0:
            out_down[...] = xs[0, 1].astype(BF16)
            store(out_down, down_h)
        else:
            back_send[...] = xs[1, 1].astype(BF16)
            back = send(back_send, back_recv, to_mirror)
        while work:
            work.pop(0)()
        if d == 1:
            store(out_out, out_h)
            store(out_in, in_h)
            yield
            back.wait_recv()
            store(back_recv, up_h)

    prepare(0)
    down = chain(0)
    next(down)
    mx.wait_recv()
    mg.wait_recv()
    prepare(1)
    up = chain(1)
    shared = gather(pl.ds(0, 2), pl.ds(2, 1))
    turn = 0
    live = [down, up]
    while live:
        for steps in list(live):
            if next(steps, "end") == "second":
                for _ in shared:
                    pass
            if steps.gi_frame is None:
                live.remove(steps)
        turn += 1
        if turn >= SHARED_AT:
            next(shared, None)
    for copy in stores:
        copy.wait()
    for copy in sent:
        copy.wait_send()


def copy_out(*refs):
    sources, results, held, sem = refs[:4], refs[4:8], refs[8:12], refs[12]
    reads = [pltpu.make_async_copy(a, b, sem.at[0, i]) for i, (a, b) in enumerate(zip(sources, held))]
    writes = [pltpu.make_async_copy(a, b, sem.at[1, i]) for i, (a, b) in enumerate(zip(held, results))]
    for copy in reads:
        copy.start()
    for read, write in zip(reads, writes):
        read.wait()
        write.start()
    for copy in writes:
        copy.wait()


def body(x_down, x_up, g_down, g_up, loss_grad, w_in, w_out, gain, retention, layer_kind):
    sections = lax.axis_size("section")
    width = w_in.shape[1]
    half, quarter = width // 2, width // 4
    anywhere = pl.BlockSpec(memory_space=pl.ANY)
    copies = 5 * AG_SEMS + 4 * (RS_SEMS + 1) + 9
    results = pl.pallas_call(
        functools.partial(kernel, sections),
        out_shape=(
            jax.ShapeDtypeStruct((4, width), BF16),
            jax.ShapeDtypeStruct((4, width), BF16),
            jax.ShapeDtypeStruct((width, 128), BF16),
            jax.ShapeDtypeStruct((128, width), BF16),
        ),
        in_specs=[anywhere] * 10,
        out_specs=(anywhere,) * 4,
        scratch_shapes=[
            pltpu.VMEM((2, 2, 4, width), BF16),
            pltpu.VMEM((2, 4, width), BF16),
            pltpu.VMEM((2, 4, width), BF16),
            pltpu.VMEM((width, 128), BF16),
            pltpu.VMEM((128, width), BF16),
            pltpu.VMEM((1, width), BF16),
            pltpu.VMEM((1, 128), BF16),
            pltpu.VMEM((1, sections), jnp.int32),
            pltpu.VMEM((4, width), BF16),
            pltpu.VMEM((4, width), BF16),
            pltpu.VMEM((4, width), BF16),
            pltpu.VMEM((width, 128), BF16),
            pltpu.VMEM((128, width), BF16),
            pltpu.SemaphoreType.DMA((8,)),
            pltpu.SemaphoreType.DMA((4,)),
            pltpu.VMEM((2, 2, 4, width), F32),
            pltpu.VMEM((2, 2, 4, width), F32),
            pltpu.VMEM((2, 4, 2, 2, XN, YN, 8, quarter), BF16),
            pltpu.VMEM((2, 2, 2, XN, YN, 8, quarter), BF16),
            pltpu.VMEM((2, 2, 2, XN, YN, 8, quarter), BF16),
            pltpu.VMEM((2, 2, 2, XN, YN, 8, quarter), BF16),
            pltpu.VMEM((2, 2, 2, YN, 8, quarter), BF16),
            pltpu.VMEM((2, 2, 3, 2, YN, 8, quarter), BF16),
            pltpu.VMEM((2, 2, 2, YN, 8, quarter), BF16),
            pltpu.VMEM((2, 2, 2, 8, quarter), BF16),
            pltpu.VMEM((2, 2, 3, 2, 8, quarter), BF16),
            pltpu.VMEM((2, 4, 4, half), BF16),
            pltpu.VMEM((2, 4, 4, half), BF16),
            pltpu.VMEM((2, 2, 4, half), F32),
            pltpu.VMEM((2, 2, 4, half), F32),
            pltpu.VMEM((2, 4, width), BF16),
            pltpu.VMEM((2, 4, width), BF16),
            pltpu.VMEM((2, 4, half), BF16),
            pltpu.VMEM((2, 4, half), BF16),
            pltpu.SemaphoreType.DMA((copies,)),
            pltpu.SemaphoreType.DMA((copies,)),
        ],
        compiler_params=pltpu.CompilerParams(
            collective_id=0, has_side_effects=True, vmem_limit_bytes=56 * 1024 * 1024
        ),
    )(
        x_down[:, 0], x_up[:, 0], g_down[0], g_up[0], loss_grad, w_in[0], w_out[0], gain, retention,
        layer_kind.reshape(1, -1),
    )
    down, up, grad_in, grad_out = pl.pallas_call(
        copy_out,
        out_shape=tuple(jax.ShapeDtypeStruct(a.shape, a.dtype) for a in results),
        in_specs=[anywhere] * 4,
        out_specs=(anywhere,) * 4,
        scratch_shapes=[pltpu.VMEM(a.shape, a.dtype) for a in results] + [pltpu.SemaphoreType.DMA((2, 4))],
    )(*results)
    return (down[None], up[None], grad_in[None], grad_out[None])


def solution(mesh):
    return jax.shard_map(
        body,
        mesh=mesh,
        in_specs=(
            P(None, "section", "tensor", None),
            P(None, "section", "tensor", None),
            P("section", "tensor", None),
            P("section", "tensor", None),
            P(None, "tensor", None),
            P("section", None, "tensor"),
            P("section", "tensor", None),
            P("section", None),
            P("section", "tensor"),
            P(),
        ),
        out_specs=(
            P("section", "tensor", None),
            P("section", "tensor", None),
            P("section", None, "tensor"),
            P("section", "tensor", None),
        ),
        check_vma=False,
    )
```

time: 1540 us -> 129 us (0.08); the launches traced: 1510 us -> 129 us
  waiting for transfers between devices: 673 us -> 0 us
  local copies, waits for them, and re-layouts: 536 us -> 0 us
  other arithmetic: 169 us -> 0 us
  Pallas kernels: 0 us -> 128 us
  starting transfers between devices: 88.5 us -> 0 us
  matrix products: 27.5 us -> 0 us
  between operations: 17.1 us -> 0.8 us
    psum x2 -> x0, waiting for transfers between devices: 562 us -> none  [layer_backward(): lax.psum(contract_last(grad_proj, w_in_l).astype(jnp.bfloat16), 'tensor')]
    rev x6 -> x0, local copies, waits for them, and re-layouts: 261 us -> none  [the longest x4 180 us: fetch_mirror(): flipped = tuple((jnp.flip(piece, 0) for piece in spread))]
    pallas_call x0 -> x2, Pallas kernels: none -> 128 us  [the longest x1 125 us: body(): pl.pallas_call(functools.partial(kernel, sections), out_shape=(jax.ShapeD...]
    unnamed x172 -> x0, local copies, waits for them, and re-layouts: 83.2 us -> none
    all_to_all x12 -> x0, starting transfers between devices: 82.3 us -> none  [the longest x4 30.8 us: fetch_mirror(): lax.all_to_all(for_sending(flatten_parts(parts, sections)), 'section', sp...]
    all_gather x8 -> x0, waiting for transfers between devices: 69.8 us -> none  [the longest x4 42.1 us: layer_backward(): lax.all_gather(normed_rows, 'tensor', axis=0, tiled=True)]
    pad x140 -> x0, local copies, waits for them, and re-layouts: 60.3 us -> none  [recurrent(): lax.associative_scan(combine_steps, (decay, (1.0 - rates) * values_in), a...]
    all_to_all x12 -> x0, other arithmetic: 59.1 us -> none  [the longest x5 20 us: fetch_mirror(): lax.all_to_all(for_sending(flipped), 'section', split_axis=0, concat_axis...]
  transfers between devices with their start and end apart: 24 -> 0, of which waited for: 11 -> 0; matrix products, arithmetic and copies ran while one was open for 40% -> 0% of each run, Pallas kernels for 0% -> 0%
where the time goes in v2:
time: 129 us
  Pallas kernels  128 us (99%)
    pallas_call x1, Pallas kernels, body(): pl.pallas_call(functools.partial(kernel, sections), out_shape=(jax.ShapeD...  125 us
    pallas_call x1, Pallas kernels, body(): pl.pallas_call(copy_out, out_shape=tuple((jax.ShapeDtypeStruct(a.shape, a...  2.65 us

profile of v2, /device:TPU:1, one launch (start us, length us, event | category | flops | bytes accessed | tf_op | source)
XLA Modules:
  0.0 128.8 jit_solution(2237728802348197113)
XLA Ops:
  0.6 125.4 %shard_map.129 = (bf16[4,4096]{1,0:T(4,128)(2,1)}, bf16[4,4096]{1,0:T(4,128)(2,1)}, bf16[4096,128]{1,0:T(8,128)(2,1)}, bf16[128,4096]{1,0:T(8,128)(2,1)}) custom-call(bf16[2,4,4096]{2,1,0:T(4,128)(2,1)} %bitcast.13, bf16[2,4,4096]{2,1,0:T(4,128)(2,1)} %bitcast.14, bf16[4,4096]{1,0:T(4,128)(2,1)} %bitcast.15, bf16[4,4096]{1,0:T(4,128)(2,1)} %bitcast.16, ...), custom_call_target="tpu_custom_call" | custom-call | tf_op jit(solution)/shard_map/pallas_call | solution.py:527
  126.0 2.6 %shard_map.130 = (bf16[4,4096]{1,0:T(4,128)(2,1)}, bf16[4,4096]{1,0:T(4,128)(2,1)}, bf16[4096,128]{1,0:T(8,128)(2,1)}, bf16[128,4096]{1,0:T(8,128)(2,1)}) custom-call(bf16[4,4096]{1,0:T(4,128)(2,1)} %get-tuple-element.12.refs_0_, bf16[4,4096]{1,0:T(4,128)(2,1)} %get-tuple-element.13.refs_1_, bf16[4096,128]{1,0:T(8,128)(2,1)} %get-tuple-element.14.refs_2_, ...), custom_call_target="tpu_custom_call" | custom-call | tf_op jit(solution)/shard_map/pallas_call | solution.py:582

commit v3 on v2

--- a/solution.py
+++ b/solution.py
@@ -326,6 +326,7 @@
                     send(p.at[0, xo, yy], xy.at[0, yy], to_xr),
                     send(p.at[1, xo, yy], xy.at[1, yy], to_xl),
                 ))
+            for yy in y_order:
                 plain.append([
                     send(p.at[1, xr, yy], xf.at[0, 1, yy], to_xr),
                     send(p.at[0, xl, yy], xf.at[1, 0, yy], to_xl),

time: 129 us -> 128 us (level)
  no operation moved by 1% of the time
where the time goes in v3:
time: 128 us
  Pallas kernels  127 us (99%)
    pallas_call x1, Pallas kernels, body(): pl.pallas_call(functools.partial(kernel, sections), out_shape=(jax.ShapeD...  125 us
    pallas_call x1, Pallas kernels, body(): pl.pallas_call(copy_out, out_shape=tuple((jax.ShapeDtypeStruct(a.shape, a...  2.65 us

profile of v3, /device:TPU:1, one launch (start us, length us, event | category | flops | bytes accessed | tf_op | source)
XLA Modules:
  0.0 128.1 jit_solution(3759635430903825482)
XLA Ops:
  0.6 124.7 %shard_map.129 = (bf16[4,4096]{1,0:T(4,128)(2,1)}, bf16[4,4096]{1,0:T(4,128)(2,1)}, bf16[4096,128]{1,0:T(8,128)(2,1)}, bf16[128,4096]{1,0:T(8,128)(2,1)}) custom-call(bf16[2,4,4096]{2,1,0:T(4,128)(2,1)} %bitcast.13, bf16[2,4,4096]{2,1,0:T(4,128)(2,1)} %bitcast.14, bf16[4,4096]{1,0:T(4,128)(2,1)} %bitcast.15, bf16[4,4096]{1,0:T(4,128)(2,1)} %bitcast.16, ...), custom_call_target="tpu_custom_call" | custom-call | tf_op jit(solution)/shard_map/pallas_call | solution.py:528
  125.3 2.6 %shard_map.130 = (bf16[4,4096]{1,0:T(4,128)(2,1)}, bf16[4,4096]{1,0:T(4,128)(2,1)}, bf16[4096,128]{1,0:T(8,128)(2,1)}, bf16[128,4096]{1,0:T(8,128)(2,1)}) custom-call(bf16[4,4096]{1,0:T(4,128)(2,1)} %get-tuple-element.12.refs_0_, bf16[4,4096]{1,0:T(4,128)(2,1)} %get-tuple-element.13.refs_1_, bf16[4096,128]{1,0:T(8,128)(2,1)} %get-tuple-element.14.refs_2_, ...), custom_call_target="tpu_custom_call" | custom-call | tf_op jit(solution)/shard_map/pallas_call | solution.py:583
